TPU v7x, 256 devices: a whole 4x4x8 slice. The times are simulated.
256 devices in a mesh: mp: 8 (over z_lo, core), dp: 8 (over z_hi, y), shard: 4 (over x).
Axes of the slice: x: 4, y: 4, z: 8 (z_hi: 2, z_lo: 4; z = z_hi * 4 + z_lo), core: 2. Of those that a mesh axis runs over, the one named last changes fastest.
Arguments:
- hidden: bfloat16 [8, 1024, 4096], P('mp', 'dp', 'shard'), may hold values from -6 to 6
- cotangent: bfloat16 [8, 1024, 14336], P('mp', 'dp', 'shard'), may hold values from -6 to 6
- weights: bfloat16 [8, 4096, 14336], P('mp', 'dp', 'shard'), may hold values from -6 to 6
- segments: int32 [8, 128], replicated, may hold values from 0 to 2, never falling along the last dimension, each value on 1 to 64 neighbouring positions
Outputs:
- merged: bfloat16 [4096, 14336], P(('dp', 'mp'), 'shard')
Inputs may be any that keep to these rules, and one draw needn't show every extreme that they name: `segments`: in every row the numbers never fall, each of the 3 numbers covers 1 to 64 tokens, and one covers exactly 64.
All inputs are finite; a program needn't handle non-finite values.
Results may differ from a plain program's by a relative error of at most 0.015.
Values may be sent and summed in bfloat16 or wider, within the bound.
A program may use at most 128 MiB of HBM per device.

v0:
```python
import math

import jax
import jax.numpy as jnp
from jax import lax
from jax.sharding import PartitionSpec as P

EX = 3
LONGEST = 64


def example_rows(segments):
    labels = jnp.arange(EX, dtype=jnp.int32)
    starts = jnp.sum((segments[:, None, :] < labels[None, :, None]).astype(jnp.int32), axis=2)
    counts = jnp.sum((segments[:, None, :] == labels[None, :, None]).astype(jnp.int32), axis=2)
    offsets = jnp.arange(LONGEST, dtype=jnp.int32)
    local = starts[:, :, None] + offsets[None, None, :]
    valid = offsets[None, None, :] < counts[:, :, None]
    return (local, valid)


def shards(hidden, cotangent, weights, segments):
    hidden_part = hidden[0]
    cotan_rows = cotangent[0]
    own_weights = weights[0]
    tokens_here = hidden_part.shape[0]
    block_rows = own_weights.shape[0]
    column_count = own_weights.shape[1]
    groups_dp = lax.axis_size("dp")
    full_states = lax.all_gather(hidden_part, "shard", axis=1, tiled=True)
    states_cols = lax.all_to_all(full_states, "dp", split_axis=1, concat_axis=0, tiled=True)
    picked = states_cols
    summed = lax.psum_scatter(
        jnp.dot(picked, own_weights, preferred_element_type=jnp.float32).astype(jnp.bfloat16),
        "dp",
        scatter_dimension=0,
        tiled=True,
    ).astype(jnp.float32)
    pre = summed * (1.0 / math.sqrt(full_states.shape[1]))
    sig = jax.nn.sigmoid(pre)
    outgrad = (cotan_rows.astype(jnp.float32) * sig * (1.0 + pre * (1.0 - sig))).astype(
        jnp.bfloat16
    )
    local, valid = example_rows(segments)
    flat_index = local.reshape(groups_dp, EX * LONGEST)
    flat_valid = valid.reshape(groups_dp, EX * LONGEST)
    padding = jnp.zeros((groups_dp, LONGEST, block_rows), jnp.bfloat16)
    padded_states = jnp.concatenate(
        [states_cols.reshape(groups_dp, tokens_here, block_rows), padding], axis=1
    )
    example_states = jnp.take_along_axis(padded_states, flat_index[:, :, None], axis=1)
    span = math.gcd(column_count, 256)
    spans = column_count // span
    piece = lax.all_gather(outgrad, "dp", axis=0, tiled=True)
    parts = piece.shape[0] // tokens_here
    zero_rows = jnp.zeros((parts, LONGEST, column_count), jnp.bfloat16)
    padded_grads = jnp.concatenate(
        [piece.reshape(parts, tokens_here, column_count), zero_rows], axis=1
    )
    picked = jnp.take_along_axis(padded_grads, flat_index[:, :, None], axis=1)
    picked = jnp.where(flat_valid[:, :, None], picked, jnp.zeros((), jnp.bfloat16))
    picked = picked.reshape(parts * EX, LONGEST, column_count)
    states_here = example_states.reshape(parts * EX, LONGEST, block_rows)

    def add_span(number, accum):
        cols = lax.dynamic_slice_in_dim(picked, number * span, span, 2)
        grads = jnp.einsum("elr,elc->erc", states_here, cols, preferred_element_type=jnp.float32)
        rounded = lax.optimization_barrier(grads.astype(jnp.bfloat16)).astype(jnp.float32)
        current = lax.dynamic_slice_in_dim(accum, number * span, span, 1)
        return lax.dynamic_update_slice_in_dim(
            accum, current + jnp.sum(rounded * rounded, axis=0), number * span, 1
        )

    fisher = lax.fori_loop(0, spans, add_span, jnp.zeros((block_rows, column_count), jnp.float32))
    numer, denom = (
        lax.psum_scatter(
            fisher * own_weights.astype(jnp.float32), "mp", scatter_dimension=0, tiled=True
        ),
        lax.psum_scatter(fisher, "mp", scatter_dimension=0, tiled=True),
    )
    return (numer / denom).astype(jnp.bfloat16)


def solution(mesh):
    return jax.shard_map(
        shards,
        mesh=mesh,
        in_specs=(P("mp", "dp", "shard"), P("mp", "dp", "shard"), P("mp", "dp", "shard"), P()),
        out_specs=P(("dp", "mp"), "shard"),
        check_vma=False,
    )
```

profile of v0, /device:TPU:2, one launch (start us, length us, event | category | flops | bytes accessed | tf_op | source)
XLA Modules:
  0.0 746.2 jit_solution(8358438577763913343)
XLA Ops:
  6.5 1.8 copy.13
  8.4 29.3 %all-gather.6.cloned.1.call-done = bf16[1,128,4096]{1,2,0:T(8,128)(2,1)} async-done(((bf16[1,128,1024]{1,2,0:T(8,128)(2,1)}), bf16[1,128,4096]{1,2,0:T(8,128)(2,1)}) %all-gather.6.cloned.1.call-update) | async-done | bytes 1048592 | tf_op jit(solution)/shard_map/all_gather | solution.py:30
  37.8 1.5 copy.14
  39.2 35.2 %all_to_all.19 = bf16[128,8,512]{2,0,1:T(8,128)(2,1)S(1)} all-to-all(bf16[128,8,512]{2,0,1:T(8,128)(2,1)S(1)} %copy.14), channel_id=1, replica_groups=mesh['mp'=8,'dp'=8,'shard'=4] {'dp'}, dimensions={1} | all-to-all | bytes 2097152 | tf_op jit(solution)/shard_map/all_to_all | solution.py:31
  74.5 8.0 %convolution_convert_fusion = bf16[1024,3584]{1,0:T(8,128)(2,1)} fusion(bf16[1024,512]{1,0:T(8,128)(2,1)S(1)} %bitcast.29, bf16[1,512,3584]{2,1,0:T(8,128)(2,1)} %param.8), kind=kOutput, calls=%fused_computation.9 | convolution fusion | flops 3761766400 | bytes 12058624 | tf_op jit(solution)/shard_map/dot_general | solution.py:34
  82.6 170.6 %reduce-scatter.4.cloned.1.call-done = bf16[128,3584]{1,0:T(8,128)(2,1)} async-done(((bf16[1024,3584]{1,0:T(8,128)(2,1)}), bf16[128,3584]{1,0:T(8,128)(2,1)}) %reduce-scatter.4.cloned.1.call-update) | async-done | bytes 917520 | tf_op jit(solution)/shard_map/reduce_scatter | solution.py:33
  253.2 3.0 fusion.4
  257.5 10.6 %gather_fusion.1 = bf16[1536,512]{1,0:T(8,128)(2,1)S(1)} fusion(bf16[8,192,512]{2,1,0:T(8,128)(2,1)S(1)} %concatenate.7, s32[1536]{0:T(1024)S(1)} %reshape.147), kind=kCustom, calls=%fused_computation.1 | custom fusion | bytes 3158016 | tf_op jit(solution)/shard_map/jit(take_along_axis)/gather | solution.py:51
  268.4 139.3 %all-gather.4.cloned.1.call-done = bf16[1024,3584]{1,0:T(8,128)(2,1)} async-done(((bf16[128,3584]{1,0:T(8,128)(2,1)}), bf16[1024,3584]{1,0:T(8,128)(2,1)}) %all-gather.4.cloned.1.call-update) | async-done | bytes 7340048 | tf_op jit(solution)/shard_map/all_gather | solution.py:54
  407.8 8.2 %concatenate.6 = bf16[8,192,3584]{2,1,0:T(8,128)(2,1)} pad(bf16[8,128,3584]{2,1,0:T(8,128)(2,1)} %bitcast.27, bf16[]{:T(256)} %constant.67.clone.1), padding=0_0x0_64x0_0 | pad | bytes 18350082 | tf_op jit(solution)/shard_map/concatenate | solution.py:57
  416.0 47.9 %gather_fusion = bf16[1536,3584]{1,0:T(8,128)(2,1)} fusion(bf16[8,192,3584]{2,1,0:T(8,128)(2,1)} %concatenate.6, s32[1536]{0:T(1024)S(1)} %reshape.147), kind=kCustom, calls=%fused_computation | custom fusion | bytes 22032384 | tf_op jit(solution)/shard_map/jit(take_along_axis)/gather | solution.py:60
  463.9 10.1 %select_select_fusion = bf16[24,64,3584]{2,1,0:T(8,128)(2,1)} fusion(bf16[24,64,3584]{2,1,0:T(8,128)(2,1)} %bitcast.26, pred[24,64]{1,0:T(8,128)(4,1)S(1)} %get-tuple-element.95, pred[24,64]{1,0:T(8,128)(4,1)S(1)} %get-tuple-element.96), kind=kLoop, calls=%fused_computation.8 | loop fusion | flops 11010048 | bytes 22023168 | tf_op jit(solution)/shard_map/jit(_where)/select_n | solution.py:61
  474.0 3.9 broadcast_in_dim.41.clone
  477.9 93.4 %while.13 = (s32[]{:T(128)}, f32[512,3584]{1,0:T(8,128)}, bf16[24,64,3584]{2,1,0:T(8,128)(2,1)}, bf16[24,64,512]{2,1,0:T(8,128)(2,1)S(1)}, s32[]{:T(128)}, /*index=5*/s32[]{:T(128)}, s32[]{:T(128)}, s32[]{:T(128)}) while((s32[]{:T(128)}, f32[512,3584]{1,0:T(8,128)}, bf16[24,64,3584]{2,1,0:T(8,128)(2,1)}, bf16[24,64,512]{2,1,0:T(8,128)(2,1)S(1)}, ...), condition=%wide.region_5.6_spmd, body=%wide.region_3.5_spmd.sunk | while | flops 415236096 | bytes 21233808 | solution.py:74
  477.9 1.1 constant_dynamic-slice_fusion.2
  479.2 3.0 convert_bitcast_fusion.2
  482.2 1.2 multiply_reduce_fusion.2
  484.6 1.1 constant_dynamic-slice_fusion.2
  485.9 3.0 convert_bitcast_fusion.2
  488.9 1.2 multiply_reduce_fusion.2
  492.5 3.0 convert_bitcast_fusion.2
  495.5 1.2 multiply_reduce_fusion.2
  499.2 3.0 convert_bitcast_fusion.2
  502.2 1.2 multiply_reduce_fusion.2
  505.9 3.0 convert_bitcast_fusion.2
  508.8 1.2 multiply_reduce_fusion.2
  512.5 3.0 convert_bitcast_fusion.2
  515.5 1.2 multiply_reduce_fusion.2
  519.1 3.0 convert_bitcast_fusion.2
  522.1 1.2 multiply_reduce_fusion.2
  525.8 3.0 convert_bitcast_fusion.2
  528.8 1.2 multiply_reduce_fusion.2
  532.5 3.0 convert_bitcast_fusion.2
  535.5 1.2 multiply_reduce_fusion.2
  539.2 3.0 convert_bitcast_fusion.2
  542.1 1.2 multiply_reduce_fusion.2
  545.8 3.0 convert_bitcast_fusion.2
  548.8 1.2 multiply_reduce_fusion.2
  552.5 3.0 convert_bitcast_fusion.2
  555.4 1.2 multiply_reduce_fusion.2
  559.2 3.0 convert_bitcast_fusion.2
  562.2 1.2 multiply_reduce_fusion.2
  565.9 3.0 convert_bitcast_fusion.2
  568.8 1.2 multiply_reduce_fusion.2
  571.4 8.2 %convert_multiply_fusion = f32[512,3584]{1,0:T(8,128)} fusion(f32[512,3584]{1,0:T(8,128)} %get-tuple-element.84, bf16[1,512,3584]{2,1,0:T(8,128)(2,1)} %param.8), kind=kLoop, calls=%fused_computation.10 | loop fusion | flops 3670016 | bytes 18350080 | tf_op jit(solution)/shard_map/mul | solution.py:77
  579.6 71.5 %reduce-scatter.8.cloned.1.call-done = f32[64,3584]{1,0:T(8,128)} async-done(((f32[512,3584]{1,0:T(8,128)}), f32[64,3584]{1,0:T(8,128)}) %reduce-scatter.8.cloned.1.call-update) | async-done | bytes 917520 | tf_op jit(solution)/shard_map/reduce_scatter | solution.py:79
  651.1 86.2 %reduce-scatter.6.cloned.1.call-done = f32[64,3584]{1,0:T(8,128)} async-done(((f32[512,3584]{1,0:T(8,128)}), f32[64,3584]{1,0:T(8,128)}) %reduce-scatter.6.cloned.1.call-update) | async-done | bytes 917520 | tf_op jit(solution)/shard_map/reduce_scatter | solution.py:76
  737.3 2.3 divide_convert_fusion
  (98 shorter events, 33.8 us)
Async XLA Ops:
  6.5 31.2 %all-gather.6.cloned.1.call-start = ((), (), s32[]{:S(2)}) async-start(), calls=%async_computation.8 | async-start | bytes 1310720 | tf_op jit(solution)/shard_map/all_gather | solution.py:30
  8.4 244.8 %reduce-scatter.4.cloned.1.call-start = ((), (), s32[]{:S(2)}) async-start(), calls=%async_computation.4 | async-start | bytes 8257536 | tf_op jit(solution)/shard_map/reduce_scatter | solution.py:33
  82.5 170.6 %copy-start = (bf16[1,128,3584]{2,1,0:T(8,128)(2,1)S(1)}, bf16[1,128,3584]{2,1,0:T(8,128)(2,1)}, u32[]{:S(2)}) copy-start(bf16[1,128,3584]{2,1,0:T(8,128)(2,1)} %param.7) | copy-start | bytes 2752516
  82.5 174.0 %copy-start.1 = (s32[8,128]{1,0:T(8,128)S(1)}, s32[8,128]{1,0:T(8,128)}, u32[]{:S(2)}) copy-start(s32[8,128]{1,0:T(8,128)} %param.9) | copy-start | bytes 12292
  82.5 325.2 %all-gather.4.cloned.1.call-start = ((), (), s32[]{:S(2)}) async-start(), calls=%async_computation.5 | async-start | bytes 8257536 | tf_op jit(solution)/shard_map/all_gather | solution.py:54
  256.1 395.0 %reduce-scatter.8.cloned.1.call-start = ((), (), s32[]{:S(2)}) async-start(), calls=%async_computation.7 | async-start | bytes 8257536 | tf_op jit(solution)/shard_map/reduce_scatter | solution.py:79
  571.3 166.0 %reduce-scatter.6.cloned.1.call-start = ((), (), s32[]{:S(2)}) async-start(), calls=%async_computation.6 | async-start | bytes 8257536 | tf_op jit(solution)/shard_map/reduce_scatter | solution.py:76
Sparse Core Ops, SparseCore 0:
  9.2 28.5 all-gather.5
  82.7 170.4 reduce-scatter.3
  256.3 151.4 all-gather.3
  571.5 79.6 reduce-scatter.7
  653.7 83.5 reduce-scatter.5
where the time goes:
time: 749 us; the launch traced here: 746 us
  waiting for transfers between devices  497 us (66%)
  local copies, waits for them, and re-layouts  108 us (14%)
  matrix products  49.7 us (7%)
  other arithmetic  42.5 us (6%)
  blocking collectives  35.2 us (5%)
  between operations  13.2 us (2%)
    reduce_scatter x1, waiting for transfers between devices, shards(): lax.psum_scatter(jnp.dot(picked, own_weights, preferred_element_type=jnp....  171 us
    all_gather x1, waiting for transfers between devices, shards(): piece = lax.all_gather(outgrad, 'dp', axis=0, tiled=True)  139 us
    reduce_scatter x1, waiting for transfers between devices, shards(): lax.psum_scatter(fisher * own_weights.astype(jnp.float32), 'mp', scatter_...  86.2 us
    reduce_scatter x1, waiting for transfers between devices, shards(): lax.psum_scatter(fisher, 'mp', scatter_dimension=0, tiled=True)  71.5 us
    gather x2, local copies, waits for them, and re-layouts, shards(): picked = jnp.take_along_axis(padded_grads, flat_index[:, :, None], axis=1)  48 us
    dot_general x14, matrix products, add_span(): jnp.einsum('elr,elc->erc', states_here, cols, preferred_element_type=jnp....  41.7 us
    all_to_all x1, blocking collectives, shards(): lax.all_to_all(full_states, 'dp', split_axis=1, concat_axis=0, tiled=True)  35.2 us
    all_gather x1, waiting for transfers between devices, shards(): full_states = lax.all_gather(hidden_part, 'shard', axis=1, tiled=True)  29.3 us
  transfers between devices with their start and end apart: 5, of which 5 were waited for; matrix products, arithmetic and copies ran while one was open for 3% of the time, Pallas kernels for 0%

commit v1 on v0

v1 whole, which is shorter than its diff:
```python
import math

import jax
import jax.numpy as jnp
from jax import lax
from jax.experimental import pallas as pl
from jax.experimental.pallas import tpu as pltpu
from jax.sharding import PartitionSpec as P

EX = 3
Y = 4
CHUNK = 256
ROWS_AT_ONCE = 64
LAG_SUM, LAG_GRAD, LAG_PASS, LAG_FISHER, LAG_CORE, LAG_NEAR, LAG_FAR = 1, 2, 3, 4, 5, 6, 7


def kernel(
    hidden, cotangent, weights, segments, out,
    w, cot, states, masked, part, part_in, own, cross, cross_in, grads, sums,
    core_in, near_in, far_in, result, fisher,
    load_sem, hid_ssem, hid_rsem, x_ssem, x_rsem, out_sem,
    part_ssem, part_rsem, cross_ssem, cross_rsem, gz_ssem, gz_rsem, gy_ssem, gy_rsem, gf_ssem, gf_rsem,
    core_ssem, core_rsem, near_ssem, near_rsem, far_ssem, far_rsem,
):
    chunks, block_rows, cw = w.shape
    tokens = cot.shape[1]
    quarter = tokens // Y
    scale = 1.0 / math.sqrt(block_rows * 2 * Y)
    mp, dp, sh = lax.axis_index("mp"), lax.axis_index("dp"), lax.axis_index("shard")
    core, b0, b1 = lax.rem(mp, 2), lax.rem(mp // 2, 2), mp // 4
    zh, y = dp // Y, lax.rem(dp, Y)

    def y_peer(d):
        return {"dp": zh * Y + lax.rem(y + d, Y)}

    def x_peer(d):
        return {"shard": lax.rem(sh + d, Y)}

    z_peer = {"dp": (1 - zh) * Y + y}
    core_peer = {"mp": mp + 1 - 2 * core}
    near_peer = {"mp": mp + 2 - 4 * b0}
    far_peer = {"mp": mp + 4 - 8 * b1}

    def remote(src, dst, ssem, rsem, device):
        return pltpu.make_async_remote_copy(
            src_ref=src,
            dst_ref=dst,
            send_sem=ssem,
            recv_sem=rsem,
            device_id=device,
            device_id_type=pl.DeviceIdType.MESH,
        )

    def load_w(c):
        cols = pl.ds(pl.multiple_of(c * cw, cw), cw)
        return pltpu.make_async_copy(weights.at[0, :, cols], w.at[c], load_sem.at[c])

    def load_cot(c):
        cols = pl.ds(pl.multiple_of(c * cw, cw), cw)
        return pltpu.make_async_copy(
            cotangent.at[0, :, cols], cot.at[c], load_sem.at[chunks + c]
        )

    def start_loads(c, carry):
        load_w(c).start()
        load_cot(c).start()
        return carry

    lax.fori_loop(0, chunks, start_loads, 0)

    barrier = pltpu.get_barrier_semaphore()

    def greet(device):
        pl.semaphore_signal(
            barrier, inc=1, device_id=device, device_id_type=pl.DeviceIdType.MESH
        )

    def from_self(j):
        return jnp.logical_and(sh == dp // 2, dp == j)

    def to_self(b, q):
        return jnp.logical_and(dp == 2 * sh + b, sh == q)

    peers = [y_peer(1), y_peer(2), y_peer(3), x_peer(1), x_peer(2), x_peer(3)]
    peers += [z_peer, core_peer, near_peer, far_peer]
    for device in peers:
        greet(device)
    for j in range(2 * Y):

        @pl.when(jnp.logical_not(from_self(j)))
        def _():
            greet({"dp": j, "shard": dp // 2})

    at_home = jnp.where(sh == dp // 2, 1, 0)
    pl.semaphore_wait(barrier, len(peers) + 2 * Y - at_home)

    def hid_send(b, q):
        return remote(
            hidden.at[0, pl.ds(q * quarter, quarter), pl.ds(b * block_rows, block_rows)],
            states.at[dp, q],
            hid_ssem.at[b * Y + q],
            hid_rsem.at[dp],
            {"dp": 2 * sh + b, "shard": q},
        )

    def hid_local(b, q):
        return pltpu.make_async_copy(
            hidden.at[0, pl.ds(q * quarter, quarter), pl.ds(b * block_rows, block_rows)],
            states.at[dp, q],
            hid_ssem.at[b * Y + q],
        )

    def hid_recv(j):
        return remote(
            states.at[j, sh], states.at[j, sh], hid_ssem.at[0], hid_rsem.at[j], {"dp": j, "shard": dp // 2}
        )

    for b in range(2):
        for q in range(Y):

            @pl.when(to_self(b, q))
            def _():
                hid_local(b, q).start()

            @pl.when(jnp.logical_not(to_self(b, q)))
            def _():
                hid_send(b, q).start()

    for j in range(2 * Y):

        @pl.when(jnp.logical_not(from_self(j)))
        def _():
            hid_recv(j).wait_recv()

    for b in range(2):
        for q in range(Y):

            @pl.when(to_self(b, q))
            def _():
                hid_local(b, q).wait()

            @pl.when(jnp.logical_not(to_self(b, q)))
            def _():
                hid_send(b, q).wait_send()

    def x_send(d):
        return remote(
            states.at[:, sh], states.at[:, sh], x_ssem.at[d - 1], x_rsem.at[d - 1], x_peer(d)
        )

    def x_recv(d):
        place = states.at[:, lax.rem(sh - d + Y, Y)]
        return remote(place, place, x_ssem.at[d - 1], x_rsem.at[d - 1], x_peer(d))

    for d in range(1, Y):
        x_send(d).start()
    for d in range(1, Y):
        x_recv(d).wait_recv()
    for d in range(1, Y):
        x_send(d).wait_send()

    def part_send(c, d):
        return remote(
            part.at[c, :, lax.rem(y + d, Y)], part_in.at[c, d - 1],
            part_ssem.at[c, d - 1], part_rsem.at[c, d - 1], y_peer(d),
        )

    def cross_send(c):
        return remote(cross.at[c], cross_in.at[c], cross_ssem.at[c], cross_rsem.at[c], z_peer)

    def gz_send(c):
        place = grads.at[c, zh, y]
        return remote(place, place, gz_ssem.at[c], gz_rsem.at[c], z_peer)

    def gz_recv(c):
        place = grads.at[c, 1 - zh, y]
        return remote(place, place, gz_ssem.at[c], gz_rsem.at[c], z_peer)

    def gy_send(c, d):
        place = grads.at[c, zh, y]
        return remote(place, place, gy_ssem.at[c, d - 1], gy_rsem.at[c, d - 1], y_peer(d))

    def gy_recv(c, d):
        place = grads.at[c, zh, lax.rem(y - d + Y, Y)]
        return remote(place, place, gy_ssem.at[c, d - 1], gy_rsem.at[c, d - 1], y_peer(d))

    def gf_send(c, d):
        place = grads.at[c, 1 - zh, y]
        return remote(place, place, gf_ssem.at[c, d - 1], gf_rsem.at[c, d - 1], y_peer(d))

    def gf_recv(c, d):
        place = grads.at[c, 1 - zh, lax.rem(y - d + Y, Y)]
        return remote(place, place, gf_ssem.at[c, d - 1], gf_rsem.at[c, d - 1], y_peer(d))

    def core_send(c):
        return remote(
            sums.at[c, 1 - core], core_in.at[c], core_ssem.at[c], core_rsem.at[c], core_peer
        )

    def near_send(c):
        return remote(
            sums.at[c, core, 1 - b0], near_in.at[c], near_ssem.at[c], near_rsem.at[c], near_peer
        )

    def far_send(c):
        return remote(
            sums.at[c, core, b0, 1 - b1], far_in.at[c], far_ssem.at[c], far_rsem.at[c], far_peer
        )

    def store(c):
        cols = pl.ds(pl.multiple_of(c * cw, cw), cw)
        return pltpu.make_async_copy(result.at[c], out.at[:, cols], out_sem.at[c])

    def product(c):
        load_w(c).wait()

        def some(j, carry):
            rows = states[j].reshape(tokens, block_rows)
            part[c, j // Y, lax.rem(j, Y)] = jnp.dot(
                rows, w[c], preferred_element_type=jnp.float32
            ).astype(jnp.bfloat16)
            return carry

        lax.fori_loop(0, 2 * Y, some, 0)
        for d in range(1, Y):
            part_send(c, d).start()

    def mask_states():
        def some(j, carry):
            rows = states[j].reshape(tokens, block_rows)
            turned = rows.astype(jnp.float32).T
            labels = segments[pl.ds(j, 1), :]
            for e in range(EX):
                masked[j * EX + e] = jnp.where(labels == e, turned, 0.0).astype(jnp.bfloat16)
            return carry

        lax.fori_loop(0, 2 * Y, some, 0)

    def add_up(c):
        for d in range(1, Y):
            part_send(c, d).wait_recv()

        def total(half):
            acc = part[c, half, y].astype(jnp.float32)
            for d in range(1, Y):
                acc += part_in[c, d - 1, half].astype(jnp.float32)
            return acc

        cross[c] = total(1 - zh).astype(jnp.bfloat16)
        cross_send(c).start()
        own[c] = total(zh)

    def gradient(c):
        load_cot(c).wait()
        cross_send(c).wait_recv()
        pre = (own[c] + cross_in[c].astype(jnp.float32)) * scale
        sig = jax.nn.sigmoid(pre)
        grads[c, zh, y] = (
            cot[c].astype(jnp.float32) * sig * (1.0 + pre * (1.0 - sig))
        ).astype(jnp.bfloat16)
        gz_send(c).start()
        for d in range(1, Y):
            gy_send(c, d).start()

    def pass_on(c):
        gz_recv(c).wait_recv()
        for d in range(1, Y):
            gf_send(c, d).start()

    def fishers(c):
        for d in range(1, Y):
            gy_recv(c, d).wait_recv()
            gf_recv(c, d).wait_recv()

        def some(r, carry):
            rows = pl.ds(pl.multiple_of(r * ROWS_AT_ONCE, ROWS_AT_ONCE), ROWS_AT_ONCE)
            acc = jnp.zeros((ROWS_AT_ONCE, cw), jnp.float32)
            for j in range(2 * Y):
                cols = grads[c, j // Y, j % Y]
                for e in range(EX):
                    grad = jnp.dot(
                        masked[j * EX + e, rows, :], cols, preferred_element_type=jnp.float32
                    )
                    acc += grad * grad
            fisher[rows, :] = acc
            return carry

        lax.fori_loop(0, block_rows // ROWS_AT_ONCE, some, 0)
        per = block_rows // 8
        for m in range(8):
            f = fisher[m * per : (m + 1) * per, :]
            at = sums.at[c, m % 2, (m // 2) % 2, m // 4]
            at[0] = (f * w[c, m * per : (m + 1) * per, :].astype(jnp.float32)).astype(jnp.bfloat16)
            at[1] = f.astype(jnp.bfloat16)
        core_send(c).start()

    def add_core(c):
        core_send(c).wait_recv()
        for i in (0, 1):
            side = b0 if i else 1 - b0
            sums[c, core, side] = (
                sums[c, core, side].astype(jnp.float32) + core_in[c, side].astype(jnp.float32)
            ).astype(jnp.bfloat16)
            if i == 0:
                near_send(c).start()

    def add_near(c):
        near_send(c).wait_recv()
        for i in (0, 1):
            side = b1 if i else 1 - b1
            sums[c, core, b0, side] = (
                sums[c, core, b0, side].astype(jnp.float32)
                + near_in[c, side].astype(jnp.float32)
            ).astype(jnp.bfloat16)
            if i == 0:
                far_send(c).start()

    def add_far(c):
        far_send(c).wait_recv()
        both = sums[c, core, b0, b1].astype(jnp.float32) + far_in[c].astype(jnp.float32)
        result[c] = (both[0] / both[1]).astype(jnp.bfloat16)
        store(c).start()

    stages = [
        (product, 0), (add_up, LAG_SUM), (gradient, LAG_GRAD), (pass_on, LAG_PASS),
        (fishers, LAG_FISHER), (add_core, LAG_CORE), (add_near, LAG_NEAR), (add_far, LAG_FAR),
    ]

    def step(t, carry):
        for stage, lag in stages:
            c = t - lag

            @pl.when(jnp.logical_and(c >= 0, c < chunks))
            def _():
                stage(c)

            if stage is product:

                @pl.when(t == 0)
                def _():
                    mask_states()

        return carry

    lax.fori_loop(0, chunks + LAG_FAR, step, 0)

    def finish(c, carry):
        for d in range(1, Y):
            part_send(c, d).wait_send()
            gy_send(c, d).wait_send()
            gf_send(c, d).wait_send()
        cross_send(c).wait_send()
        gz_send(c).wait_send()
        core_send(c).wait_send()
        near_send(c).wait_send()
        far_send(c).wait_send()
        store(c).wait()
        return carry

    lax.fori_loop(0, chunks, finish, 0)


def shards(hidden, cotangent, weights, segments):
    tokens, block_rows, columns = hidden.shape[1], weights.shape[1], weights.shape[2]
    cw = CHUNK
    n = columns // cw
    per = block_rows // 8
    bf, f32 = jnp.bfloat16, jnp.float32
    dma = pltpu.SemaphoreType.DMA
    buffers = [
        pltpu.VMEM((n, block_rows, cw), bf),
        pltpu.VMEM((n, tokens, cw), bf),
        pltpu.VMEM((2 * Y, Y, tokens // Y, block_rows), bf),
        pltpu.VMEM((2 * Y * EX, block_rows, tokens), bf),
        pltpu.VMEM((n, 2, Y, tokens, cw), bf),
        pltpu.VMEM((n, Y - 1, 2, tokens, cw), bf),
        pltpu.VMEM((n, tokens, cw), f32),
        pltpu.VMEM((n, tokens, cw), bf),
        pltpu.VMEM((n, tokens, cw), bf),
        pltpu.VMEM((n, 2, Y, tokens, cw), bf),
        pltpu.VMEM((n, 2, 2, 2, 2, per, cw), bf),
        pltpu.VMEM((n, 2, 2, 2, per, cw), bf),
        pltpu.VMEM((n, 2, 2, per, cw), bf),
        pltpu.VMEM((n, 2, per, cw), bf),
        pltpu.VMEM((n, per, cw), bf),
        pltpu.VMEM((block_rows, cw), f32),
    ]
    many = [dma((n, Y - 1))] * 2
    one = [dma((n,))] * 2
    sems = [dma((2 * n,)), dma((2 * Y,)), dma((2 * Y,)), dma((Y - 1,)), dma((Y - 1,)), dma((n,))]
    sems += many + one + one + many + many + one + one + one
    return pl.pallas_call(
        kernel,
        out_shape=jax.ShapeDtypeStruct((per, columns), bf),
        in_specs=[pl.BlockSpec(memory_space=pl.ANY)] * 3
        + [pl.BlockSpec(memory_space=pltpu.VMEM)],
        out_specs=pl.BlockSpec(memory_space=pl.ANY),
        scratch_shapes=buffers + sems,
        compiler_params=pltpu.CompilerParams(
            collective_id=0, has_side_effects=True, vmem_limit_bytes=60 * 2**20
        ),
    )(hidden, cotangent, weights, segments)


def solution(mesh):
    return jax.shard_map(
        shards,
        mesh=mesh,
        in_specs=(P("mp", "dp", "shard"), P("mp", "dp", "shard"), P("mp", "dp", "shard"), P()),
        out_specs=P(("dp", "mp"), "shard"),
        check_vma=False,
    )
```

time: 749 us -> 230 us (0.31)
  waiting for transfers between devices: 497 us -> 0 us
  Pallas kernels: 0 us -> 225 us
  local copies, waits for them, and re-layouts: 108 us -> 1.82 us
  matrix products: 49.7 us -> 0 us
  other arithmetic: 42.5 us -> 0 us
  blocking collectives: 35.2 us -> 0 us
  between operations: 13.2 us -> 0.01 us
    reduce_scatter x3 -> x0, waiting for transfers between devices: 328 us -> none  [the longest x1 171 us: shards(): lax.psum_scatter(jnp.dot(picked, own_weights, preferred_element_type=jnp....]
    pallas_call x0 -> x1, Pallas kernels: none -> 225 us  [shards(): pl.pallas_call(kernel, out_shape=jax.ShapeDtypeStruct((per, columns), bf)...]
    all_gather x2 -> x0, waiting for transfers between devices: 169 us -> none  [the longest x1 139 us: shards(): piece = lax.all_gather(outgrad, 'dp', axis=0, tiled=True)]
    gather x3 -> x0, local copies, waits for them, and re-layouts: 58.6 us -> none  [the longest x2 48 us: shards(): picked = jnp.take_along_axis(padded_grads, flat_index[:, :, None], axis=1)]
    dot_general x15 -> x0, matrix products: 49.7 us -> none  [the longest x14 41.7 us: add_span(): jnp.einsum('elr,elc->erc', states_here, cols, preferred_element_type=jnp....]
    all_to_all x1 -> x0, blocking collectives: 35.2 us -> none  [shards(): lax.all_to_all(full_states, 'dp', split_axis=1, concat_axis=0, tiled=True)]
    dynamic_slice x28 -> x0, local copies, waits for them, and re-layouts: 17.8 us -> none  [add_span(): current = lax.dynamic_slice_in_dim(accum, number * span, span, 1)]
    reduce_sum x15 -> x0, other arithmetic: 17.3 us -> none  [the longest x14 17.2 us: add_span(): jnp.sum(rounded * rounded, axis=0)]
  transfers between devices with their start and end apart: 5 -> 0, of which waited for: 5 -> 0; matrix products, arithmetic and copies ran while one was open for 3% -> 0% of each run, Pallas kernels for 0% -> 0%
where the time goes in v1:
time: 230 us; the launch traced here: 227 us
  Pallas kernels  225 us (98%)
    pallas_call x1, Pallas kernels, shards(): pl.pallas_call(kernel, out_shape=jax.ShapeDtypeStruct((per, columns), bf)...  225 us

profile of v1, /device:TPU:2, one launch (start us, length us, event | category | flops | bytes accessed | tf_op | source)
XLA Modules:
  0.0 227.2 jit_solution(419276226645722161)
XLA Ops:
  0.0 225.4 %shard_map.46 = bf16[64,3584]{1,0:T(8,128)(2,1)} custom-call(bf16[1,128,1024]{2,1,0:T(8,128)(2,1)} %hidden.1, bf16[1,128,3584]{2,1,0:T(8,128)(2,1)} %cotangent.1, bf16[1,512,3584]{2,1,0:T(8,128)(2,1)} %weights.1, s32[8,128]{1,0:T(8,128)} %segments.1), custom_call_target="tpu_custom_call" | custom-call | tf_op jit(solution)/shard_map/pallas_call | solution.py:392
  225.4 1.8 copy.6

commit v2 on v1

--- a/solution.py
+++ b/solution.py
@@ -11,15 +11,17 @@
 Y = 4
 CHUNK = 256
 ROWS_AT_ONCE = 64
-LAG_SUM, LAG_GRAD, LAG_PASS, LAG_FISHER, LAG_CORE, LAG_NEAR, LAG_FAR = 1, 2, 3, 4, 5, 6, 7
+LAG_HALF, LAG_SUM, LAG_GRAD, LAG_PASS, LAG_RELAY = 1, 2, 3, 4, 5
+LAG_FISHER, LAG_CORE, LAG_NEAR, LAG_FAR = 6, 7, 8, 9
 
 
 def kernel(
     hidden, cotangent, weights, segments, out,
-    w, cot, states, masked, part, part_in, own, cross, cross_in, grads, sums,
+    w, cot, states, masked, part, half_in, part_in, own, cross, cross_in, grads, sums,
     core_in, near_in, far_in, result, fisher,
     load_sem, hid_ssem, hid_rsem, x_ssem, x_rsem, out_sem,
-    part_ssem, part_rsem, cross_ssem, cross_rsem, gz_ssem, gz_rsem, gy_ssem, gy_rsem, gf_ssem, gf_rsem,
+    half_ssem, half_rsem, soon_ssem, soon_rsem, late_ssem, late_rsem, cross_ssem, cross_rsem,
+    gz_ssem, gz_rsem, gy_ssem, gy_rsem, relay_ssem, relay_rsem,
     core_ssem, core_rsem, near_ssem, near_rsem, far_ssem, far_rsem,
 ):
     chunks, block_rows, cw = w.shape
@@ -81,7 +83,7 @@
     def to_self(b, q):
         return jnp.logical_and(dp == 2 * sh + b, sh == q)
 
-    peers = [y_peer(1), y_peer(2), y_peer(3), x_peer(1), x_peer(2), x_peer(3)]
+    peers = [y_peer(1), y_peer(3), x_peer(1), x_peer(2), x_peer(3)]
     peers += [z_peer, core_peer, near_peer, far_peer]
     for device in peers:
         greet(device)
@@ -126,43 +128,63 @@
             def _():
                 hid_send(b, q).start()
 
-    for j in range(2 * Y):
-
-        @pl.when(jnp.logical_not(from_self(j)))
-        def _():
-            hid_recv(j).wait_recv()
-
-    for b in range(2):
-        for q in range(Y):
-
-            @pl.when(to_self(b, q))
-            def _():
-                hid_local(b, q).wait()
-
-            @pl.when(jnp.logical_not(to_self(b, q)))
-            def _():
-                hid_send(b, q).wait_send()
-
-    def x_send(d):
-        return remote(
-            states.at[:, sh], states.at[:, sh], x_ssem.at[d - 1], x_rsem.at[d - 1], x_peer(d)
-        )
-
-    def x_recv(d):
-        place = states.at[:, lax.rem(sh - d + Y, Y)]
-        return remote(place, place, x_ssem.at[d - 1], x_rsem.at[d - 1], x_peer(d))
-
-    for d in range(1, Y):
-        x_send(d).start()
-    for d in range(1, Y):
-        x_recv(d).wait_recv()
-    for d in range(1, Y):
-        x_send(d).wait_send()
-
-    def part_send(c, d):
-        return remote(
-            part.at[c, :, lax.rem(y + d, Y)], part_in.at[c, d - 1],
-            part_ssem.at[c, d - 1], part_rsem.at[c, d - 1], y_peer(d),
+    def x_send(side, d):
+        place = states.at[pl.ds(side * Y, Y), sh]
+        at = side * (Y - 1) + d - 1
+        return remote(place, place, x_ssem.at[at], x_rsem.at[at], x_peer(d))
+
+    def x_recv(side, d):
+        place = states.at[pl.ds(side * Y, Y), lax.rem(sh - d + Y, Y)]
+        at = side * (Y - 1) + d - 1
+        return remote(place, place, x_ssem.at[at], x_rsem.at[at], x_peer(d))
+
+    def x_forward(side):
+        for i in range(Y):
+            j = side * Y + i
+
+            @pl.when(jnp.logical_not(from_self(j)))
+            def _():
+                hid_recv(j).wait_recv()
+
+            @pl.when(from_self(j))
+            def _():
+                hid_local(lax.rem(dp, 2), sh).wait()
+
+        for d in range(1, Y):
+            x_send(side, d).start()
+
+    x_forward(zh)
+    x_forward(1 - zh)
+    for side in (zh, 1 - zh):
+        for d in range(1, Y):
+            x_recv(side, d).wait_recv()
+
+    half = tokens // 2
+
+    def y_next(i):
+        return lax.rem(y + (1, Y - 1)[i], Y)
+
+    def y_to(i):
+        return y_peer((1, Y - 1)[i])
+
+    def half_send(c, i):
+        return remote(
+            part.at[c, :, lax.rem(y + 2, Y), pl.ds(i * half, half)], half_in.at[c, i],
+            half_ssem.at[c, i], half_rsem.at[c, i], y_to(i),
+        )
+
+    def soon_send(c, i):
+        rows = pl.ds((1 - i) * half, half)
+        return remote(
+            part.at[c, :, y_next(i), rows], part_in.at[c, i, :, rows],
+            soon_ssem.at[c, i], soon_rsem.at[c, i], y_to(i),
+        )
+
+    def late_send(c, i):
+        rows = pl.ds(i * half, half)
+        return remote(
+            part.at[c, :, y_next(i), rows], part_in.at[c, i, :, rows],
+            late_ssem.at[c, i], late_rsem.at[c, i], y_to(i),
         )
 
     def cross_send(c):
@@ -176,21 +198,25 @@
         place = grads.at[c, 1 - zh, y]
         return remote(place, place, gz_ssem.at[c], gz_rsem.at[c], z_peer)
 
-    def gy_send(c, d):
-        place = grads.at[c, zh, y]
-        return remote(place, place, gy_ssem.at[c, d - 1], gy_rsem.at[c, d - 1], y_peer(d))
-
-    def gy_recv(c, d):
-        place = grads.at[c, zh, lax.rem(y - d + Y, Y)]
-        return remote(place, place, gy_ssem.at[c, d - 1], gy_rsem.at[c, d - 1], y_peer(d))
-
-    def gf_send(c, d):
-        place = grads.at[c, 1 - zh, y]
-        return remote(place, place, gf_ssem.at[c, d - 1], gf_rsem.at[c, d - 1], y_peer(d))
-
-    def gf_recv(c, d):
-        place = grads.at[c, 1 - zh, lax.rem(y - d + Y, Y)]
-        return remote(place, place, gf_ssem.at[c, d - 1], gf_rsem.at[c, d - 1], y_peer(d))
+    def gy_send(c, side, i):
+        place = grads.at[c, side, y]
+        at = 2 * side + i
+        return remote(place, place, gy_ssem.at[c, at], gy_rsem.at[c, at], y_to(i))
+
+    def gy_recv(c, side, i):
+        place = grads.at[c, side, y_next(1 - i)]
+        at = 2 * side + i
+        return remote(place, place, gy_ssem.at[c, at], gy_rsem.at[c, at], y_to(i))
+
+    def relay_send(c, side, i):
+        place = grads.at[c, side, y_next(1 - i), pl.ds(i * half, half)]
+        at = 2 * side + i
+        return remote(place, place, relay_ssem.at[c, at], relay_rsem.at[c, at], y_to(i))
+
+    def relay_recv(c, side, i):
+        place = grads.at[c, side, lax.rem(y + 2, Y), pl.ds(i * half, half)]
+        at = 2 * side + i
+        return remote(place, place, relay_ssem.at[c, at], relay_rsem.at[c, at], y_to(i))
 
     def core_send(c):
         return remote(
@@ -222,8 +248,20 @@
             return carry
 
         lax.fori_loop(0, 2 * Y, some, 0)
-        for d in range(1, Y):
-            part_send(c, d).start()
+        for i in range(2):
+            half_send(c, i).start()
+        for i in range(2):
+            soon_send(c, i).start()
+
+    def add_half(c):
+        for i in range(2):
+            half_send(c, i).wait_recv()
+            rows = pl.ds(i * half, half)
+            part[c, :, y_next(i), rows] = (
+                part[c, :, y_next(i), rows].astype(jnp.float32)
+                + half_in[c, i].astype(jnp.float32)
+            ).astype(jnp.bfloat16)
+            late_send(c, i).start()
 
     def mask_states():
         def some(j, carry):
@@ -237,13 +275,14 @@
         lax.fori_loop(0, 2 * Y, some, 0)
 
     def add_up(c):
-        for d in range(1, Y):
-            part_send(c, d).wait_recv()
-
-        def total(half):
-            acc = part[c, half, y].astype(jnp.float32)
-            for d in range(1, Y):
-                acc += part_in[c, d - 1, half].astype(jnp.float32)
+        for i in range(2):
+            soon_send(c, i).wait_recv()
+            late_send(c, i).wait_recv()
+
+        def total(side):
+            acc = part[c, side, y].astype(jnp.float32)
+            for i in range(2):
+                acc += part_in[c, i, side].astype(jnp.float32)
             return acc
 
         cross[c] = total(1 - zh).astype(jnp.bfloat16)
@@ -259,18 +298,27 @@
             cot[c].astype(jnp.float32) * sig * (1.0 + pre * (1.0 - sig))
         ).astype(jnp.bfloat16)
         gz_send(c).start()
-        for d in range(1, Y):
-            gy_send(c, d).start()
+        for i in range(2):
+            gy_send(c, zh, i).start()
+
+    def relay(c, side):
+        for i in range(2):
+            gy_recv(c, side, i).wait_recv()
+            relay_send(c, side, i).start()
 
     def pass_on(c):
         gz_recv(c).wait_recv()
-        for d in range(1, Y):
-            gf_send(c, d).start()
+        for i in range(2):
+            gy_send(c, 1 - zh, i).start()
+        relay(c, zh)
+
+    def relay_far(c):
+        relay(c, 1 - zh)
 
     def fishers(c):
-        for d in range(1, Y):
-            gy_recv(c, d).wait_recv()
-            gf_recv(c, d).wait_recv()
+        for side in range(2):
+            for i in range(2):
+                relay_recv(c, side, i).wait_recv()
 
         def some(r, carry):
             rows = pl.ds(pl.multiple_of(r * ROWS_AT_ONCE, ROWS_AT_ONCE), ROWS_AT_ONCE)
@@ -322,7 +370,8 @@
         store(c).start()
 
     stages = [
-        (product, 0), (add_up, LAG_SUM), (gradient, LAG_GRAD), (pass_on, LAG_PASS),
+        (product, 0), (add_half, LAG_HALF), (add_up, LAG_SUM), (gradient, LAG_GRAD),
+        (pass_on, LAG_PASS), (relay_far, LAG_RELAY),
         (fishers, LAG_FISHER), (add_core, LAG_CORE), (add_near, LAG_NEAR), (add_far, LAG_FAR),
     ]
 
@@ -344,11 +393,25 @@
 
     lax.fori_loop(0, chunks + LAG_FAR, step, 0)
 
+    for b in range(2):
+        for q in range(Y):
+
+            @pl.when(jnp.logical_not(to_self(b, q)))
+            def _():
+                hid_send(b, q).wait_send()
+
+    for side in range(2):
+        for d in range(1, Y):
+            x_send(side, d).wait_send()
+
     def finish(c, carry):
-        for d in range(1, Y):
-            part_send(c, d).wait_send()
-            gy_send(c, d).wait_send()
-            gf_send(c, d).wait_send()
+        for i in range(2):
+            half_send(c, i).wait_send()
+            soon_send(c, i).wait_send()
+            late_send(c, i).wait_send()
+            for side in range(2):
+                gy_send(c, side, i).wait_send()
+                relay_send(c, side, i).wait_send()
         cross_send(c).wait_send()
         gz_send(c).wait_send()
         core_send(c).wait_send()
@@ -373,7 +436,8 @@
         pltpu.VMEM((2 * Y, Y, tokens // Y, block_rows), bf),
         pltpu.VMEM((2 * Y * EX, block_rows, tokens), bf),
         pltpu.VMEM((n, 2, Y, tokens, cw), bf),
-        pltpu.VMEM((n, Y - 1, 2, tokens, cw), bf),
+        pltpu.VMEM((n, 2, 2, tokens // 2, cw), bf),
+        pltpu.VMEM((n, 2, 2, tokens, cw), bf),
         pltpu.VMEM((n, tokens, cw), f32),
         pltpu.VMEM((n, tokens, cw), bf),
         pltpu.VMEM((n, tokens, cw), bf),
@@ -385,10 +449,10 @@
         pltpu.VMEM((n, per, cw), bf),
         pltpu.VMEM((block_rows, cw), f32),
     ]
-    many = [dma((n, Y - 1))] * 2
-    one = [dma((n,))] * 2
-    sems = [dma((2 * n,)), dma((2 * Y,)), dma((2 * Y,)), dma((Y - 1,)), dma((Y - 1,)), dma((n,))]
-    sems += many + one + one + many + many + one + one + one
+    one, two, four = ([dma((n,) + more)] * 2 for more in ((), (2,), (4,)))
+    crossing = [dma((2 * Y,))] * 2 + [dma((2 * (Y - 1),))] * 2
+    sems = [dma((2 * n,))] + crossing + [dma((n,))]
+    sems += two + two + two + one + one + four + four + one + one + one
     return pl.pallas_call(
         kernel,
         out_shape=jax.ShapeDtypeStruct((per, columns), bf),

time: 230 us -> 206 us (0.90)
  Pallas kernels: 225 us -> 204 us
    pallas_call x1, Pallas kernels: 225 us -> 204 us  [shards(): pl.pallas_call(kernel, out_shape=jax.ShapeDtypeStruct((per, columns), bf)...]
where the time goes in v2:
time: 206 us; the launch traced here: 205 us
  Pallas kernels  204 us (99%)
    pallas_call x1, Pallas kernels, shards(): pl.pallas_call(kernel, out_shape=jax.ShapeDtypeStruct((per, columns), bf)...  204 us

profile of v2, /device:TPU:2, one launch (start us, length us, event | category | flops | bytes accessed | tf_op | source)
XLA Modules:
  0.0 205.5 jit_solution(9597188985491268925)
XLA Ops:
  0.0 203.6 %shard_map.46 = bf16[64,3584]{1,0:T(8,128)(2,1)} custom-call(bf16[1,128,1024]{2,1,0:T(8,128)(2,1)} %hidden.1, bf16[1,128,3584]{2,1,0:T(8,128)(2,1)} %cotangent.1, bf16[1,512,3584]{2,1,0:T(8,128)(2,1)} %weights.1, s32[8,128]{1,0:T(8,128)} %segments.1), custom_call_target="tpu_custom_call" | custom-call | tf_op jit(solution)/shard_map/pallas_call | solution.py:456
  203.6 1.8 copy.6

commit v3 on v2

--- a/solution.py
+++ b/solution.py
@@ -11,8 +11,8 @@
 Y = 4
 CHUNK = 256
 ROWS_AT_ONCE = 64
-LAG_HALF, LAG_SUM, LAG_GRAD, LAG_PASS, LAG_RELAY = 1, 2, 3, 4, 5
-LAG_FISHER, LAG_CORE, LAG_NEAR, LAG_FAR = 6, 7, 8, 9
+LAG_HALF, LAG_SUM, LAG_GRAD, LAG_PASS, LAG_RELAY = 1, 2, 4, 6, 7
+LAG_FISHER, LAG_CORE, LAG_NEAR, LAG_FAR = 8, 9, 10, 11
 
 
 def kernel(
@@ -128,36 +128,32 @@
             def _():
                 hid_send(b, q).start()
 
-    def x_send(side, d):
-        place = states.at[pl.ds(side * Y, Y), sh]
-        at = side * (Y - 1) + d - 1
-        return remote(place, place, x_ssem.at[at], x_rsem.at[at], x_peer(d))
-
-    def x_recv(side, d):
-        place = states.at[pl.ds(side * Y, Y), lax.rem(sh - d + Y, Y)]
-        at = side * (Y - 1) + d - 1
-        return remote(place, place, x_ssem.at[at], x_rsem.at[at], x_peer(d))
-
-    def x_forward(side):
+    def x_send(j, d):
+        place = states.at[j, sh]
+        return remote(place, place, x_ssem.at[d - 1], x_rsem.at[j, d - 1], x_peer(d))
+
+    def x_recv(j, d):
+        place = states.at[j, lax.rem(sh - d + Y, Y)]
+        return remote(place, place, x_ssem.at[d - 1], x_rsem.at[j, d - 1], x_peer(d))
+
+    def x_forward(j):
+        @pl.when(jnp.logical_not(from_self(j)))
+        def _():
+            hid_recv(j).wait_recv()
+
+        @pl.when(from_self(j))
+        def _():
+            hid_local(lax.rem(dp, 2), sh).wait()
+
+        for d in range(1, Y):
+            x_send(j, d).start()
+
+    for side in (zh, 1 - zh):
         for i in range(Y):
-            j = side * Y + i
-
-            @pl.when(jnp.logical_not(from_self(j)))
-            def _():
-                hid_recv(j).wait_recv()
-
-            @pl.when(from_self(j))
-            def _():
-                hid_local(lax.rem(dp, 2), sh).wait()
-
+            x_forward(side * Y + i)
+    for j in range(2 * Y):
         for d in range(1, Y):
-            x_send(side, d).start()
-
-    x_forward(zh)
-    x_forward(1 - zh)
-    for side in (zh, 1 - zh):
-        for d in range(1, Y):
-            x_recv(side, d).wait_recv()
+            x_recv(j, d).wait_recv()
 
     half = tokens // 2
 
@@ -170,67 +166,67 @@
     def half_send(c, i):
         return remote(
             part.at[c, :, lax.rem(y + 2, Y), pl.ds(i * half, half)], half_in.at[c, i],
-            half_ssem.at[c, i], half_rsem.at[c, i], y_to(i),
+            half_ssem, half_rsem.at[c, i], y_to(i),
         )
 
     def soon_send(c, i):
         rows = pl.ds((1 - i) * half, half)
         return remote(
             part.at[c, :, y_next(i), rows], part_in.at[c, i, :, rows],
-            soon_ssem.at[c, i], soon_rsem.at[c, i], y_to(i),
+            soon_ssem, soon_rsem.at[c, i], y_to(i),
         )
 
     def late_send(c, i):
         rows = pl.ds(i * half, half)
         return remote(
             part.at[c, :, y_next(i), rows], part_in.at[c, i, :, rows],
-            late_ssem.at[c, i], late_rsem.at[c, i], y_to(i),
+            late_ssem, late_rsem.at[c, i], y_to(i),
         )
 
     def cross_send(c):
-        return remote(cross.at[c], cross_in.at[c], cross_ssem.at[c], cross_rsem.at[c], z_peer)
+        return remote(cross.at[c], cross_in.at[c], cross_ssem, cross_rsem.at[c], z_peer)
 
     def gz_send(c):
         place = grads.at[c, zh, y]
-        return remote(place, place, gz_ssem.at[c], gz_rsem.at[c], z_peer)
+        return remote(place, place, gz_ssem, gz_rsem.at[c], z_peer)
 
     def gz_recv(c):
         place = grads.at[c, 1 - zh, y]
-        return remote(place, place, gz_ssem.at[c], gz_rsem.at[c], z_peer)
+        return remote(place, place, gz_ssem, gz_rsem.at[c], z_peer)
 
     def gy_send(c, side, i):
         place = grads.at[c, side, y]
         at = 2 * side + i
-        return remote(place, place, gy_ssem.at[c, at], gy_rsem.at[c, at], y_to(i))
+        return remote(place, place, gy_ssem, gy_rsem.at[c, at], y_to(i))
 
     def gy_recv(c, side, i):
         place = grads.at[c, side, y_next(1 - i)]
         at = 2 * side + i
-        return remote(place, place, gy_ssem.at[c, at], gy_rsem.at[c, at], y_to(i))
+        return remote(place, place, gy_ssem, gy_rsem.at[c, at], y_to(i))
 
     def relay_send(c, side, i):
         place = grads.at[c, side, y_next(1 - i), pl.ds(i * half, half)]
         at = 2 * side + i
-        return remote(place, place, relay_ssem.at[c, at], relay_rsem.at[c, at], y_to(i))
+        return remote(place, place, relay_ssem, relay_rsem.at[c, at], y_to(i))
 
     def relay_recv(c, side, i):
         place = grads.at[c, side, lax.rem(y + 2, Y), pl.ds(i * half, half)]
         at = 2 * side + i
-        return remote(place, place, relay_ssem.at[c, at], relay_rsem.at[c, at], y_to(i))
+        return remote(place, place, relay_ssem, relay_rsem.at[c, at], y_to(i))
 
     def core_send(c):
         return remote(
-            sums.at[c, 1 - core], core_in.at[c], core_ssem.at[c], core_rsem.at[c], core_peer
+            sums.at[c, 1 - core], core_in.at[c], core_ssem, core_rsem.at[c], core_peer
         )
 
     def near_send(c):
         return remote(
-            sums.at[c, core, 1 - b0], near_in.at[c], near_ssem.at[c], near_rsem.at[c], near_peer
+            sums.at[c, core, 1 - b0], near_in.at[c], near_ssem, near_rsem.at[c], near_peer
         )
 
     def far_send(c):
         return remote(
-            sums.at[c, core, b0, 1 - b1], far_in.at[c], far_ssem.at[c], far_rsem.at[c], far_peer
+            sums.at[c, core, b0, 1 - b1], far_in.at[c], far_ssem, far_rsem.at[c], far_peer
         )
 
     def store(c):
@@ -263,7 +259,7 @@
             ).astype(jnp.bfloat16)
             late_send(c, i).start()
 
-    def mask_states():
+    def mask_states(first, last):
         def some(j, carry):
             rows = states[j].reshape(tokens, block_rows)
             turned = rows.astype(jnp.float32).T
@@ -272,7 +268,7 @@
                 masked[j * EX + e] = jnp.where(labels == e, turned, 0.0).astype(jnp.bfloat16)
             return carry
 
-        lax.fori_loop(0, 2 * Y, some, 0)
+        lax.fori_loop(first, last, some, 0)
 
     def add_up(c):
         for i in range(2):
@@ -383,11 +379,9 @@
             def _():
                 stage(c)
 
-            if stage is product:
-
-                @pl.when(t == 0)
-                def _():
-                    mask_states()
+        @pl.when(jnp.logical_and(t >= 1, t <= Y))
+        def _():
+            mask_states(2 * t - 2, 2 * t)
 
         return carry
 
@@ -400,23 +394,23 @@
             def _():
                 hid_send(b, q).wait_send()
 
-    for side in range(2):
-        for d in range(1, Y):
-            x_send(side, d).wait_send()
+    def sent(ref, ssem):
+        remote(ref, ref, ssem, cross_rsem.at[0], z_peer).wait_send()
+
+    for i in range(1, Y):
+        sent(states.at[:, 0], x_ssem.at[i - 1])
+    sent(half_in, half_ssem)
+    sent(half_in, soon_ssem)
+    sent(half_in, late_ssem)
+    sent(cross, cross_ssem)
+    sent(cross, gz_ssem)
+    sent(part_in, gy_ssem)
+    sent(half_in, relay_ssem)
+    sent(core_in, core_ssem)
+    sent(near_in, near_ssem)
+    sent(far_in, far_ssem)
 
     def finish(c, carry):
-        for i in range(2):
-            half_send(c, i).wait_send()
-            soon_send(c, i).wait_send()
-            late_send(c, i).wait_send()
-            for side in range(2):
-                gy_send(c, side, i).wait_send()
-                relay_send(c, side, i).wait_send()
-        cross_send(c).wait_send()
-        gz_send(c).wait_send()
-        core_send(c).wait_send()
-        near_send(c).wait_send()
-        far_send(c).wait_send()
         store(c).wait()
         return carry
 
@@ -449,8 +443,8 @@
         pltpu.VMEM((n, per, cw), bf),
         pltpu.VMEM((block_rows, cw), f32),
     ]
-    one, two, four = ([dma((n,) + more)] * 2 for more in ((), (2,), (4,)))
-    crossing = [dma((2 * Y,))] * 2 + [dma((2 * (Y - 1),))] * 2
+    one, two, four = ([dma, dma((n,) + more)] for more in ((), (2,), (4,)))
+    crossing = [dma((2 * Y,))] * 2 + [dma((Y - 1,)), dma((2 * Y, Y - 1))]
     sems = [dma((2 * n,))] + crossing + [dma((n,))]
     sems += two + two + two + one + one + four + four + one + one + one
     return pl.pallas_call(

time: 206 us -> 200 us (0.971)
  Pallas kernels: 204 us -> 197 us
    pallas_call x1, Pallas kernels: 204 us -> 197 us  [shards(): pl.pallas_call(kernel, out_shape=jax.ShapeDtypeStruct((per, columns), bf)...]
where the time goes in v3:
time: 200 us; the launch traced here: 199 us
  Pallas kernels  197 us (98%)
    pallas_call x1, Pallas kernels, shards(): pl.pallas_call(kernel, out_shape=jax.ShapeDtypeStruct((per, columns), bf)...  197 us

profile of v3, /device:TPU:2, one launch (start us, length us, event | category | flops | bytes accessed | tf_op | source)
XLA Modules:
  0.0 199.3 jit_solution(1421603915190250796)
XLA Ops:
  0.0 197.4 %shard_map.46 = bf16[64,3584]{1,0:T(8,128)(2,1)} custom-call(bf16[1,128,1024]{2,1,0:T(8,128)(2,1)} %hidden.1, bf16[1,128,3584]{2,1,0:T(8,128)(2,1)} %cotangent.1, bf16[1,512,3584]{2,1,0:T(8,128)(2,1)} %weights.1, s32[8,128]{1,0:T(8,128)} %segments.1), custom_call_target="tpu_custom_call" | custom-call | tf_op jit(solution)/shard_map/pallas_call | solution.py:450
  197.4 1.8 copy.6

commit v4 on v3

--- a/solution.py
+++ b/solution.py
@@ -19,13 +19,13 @@
     hidden, cotangent, weights, segments, out,
     w, cot, states, masked, part, half_in, part_in, own, cross, cross_in, grads, sums,
     core_in, near_in, far_in, result, fisher,
-    load_sem, hid_ssem, hid_rsem, x_ssem, x_rsem, out_sem,
-    half_ssem, half_rsem, soon_ssem, soon_rsem, late_ssem, late_rsem, cross_ssem, cross_rsem,
+    load_sem, cot_sem, hid_ssem, hid_rsem, x_ssem, x_rsem, out_sem,
+    half_ssem, half_rsem, part_ssem, part_rsem, cross_ssem, cross_rsem,
     gz_ssem, gz_rsem, gy_ssem, gy_rsem, relay_ssem, relay_rsem,
     core_ssem, core_rsem, near_ssem, near_rsem, far_ssem, far_rsem,
 ):
     chunks, block_rows, cw = w.shape
-    tokens = cot.shape[1]
+    tokens = cot.shape[0]
     quarter = tokens // Y
     scale = 1.0 / math.sqrt(block_rows * 2 * Y)
     mp, dp, sh = lax.axis_index("mp"), lax.axis_index("dp"), lax.axis_index("shard")
@@ -57,17 +57,13 @@
         cols = pl.ds(pl.multiple_of(c * cw, cw), cw)
         return pltpu.make_async_copy(weights.at[0, :, cols], w.at[c], load_sem.at[c])
 
-    def load_cot(c):
-        cols = pl.ds(pl.multiple_of(c * cw, cw), cw)
-        return pltpu.make_async_copy(
-            cotangent.at[0, :, cols], cot.at[c], load_sem.at[chunks + c]
-        )
+    load_cot = pltpu.make_async_copy(cotangent.at[0], cot, cot_sem)
 
     def start_loads(c, carry):
         load_w(c).start()
-        load_cot(c).start()
         return carry
 
+    load_cot.start()
     lax.fori_loop(0, chunks, start_loads, 0)
 
     barrier = pltpu.get_barrier_semaphore()
@@ -130,11 +126,7 @@
 
     def x_send(j, d):
         place = states.at[j, sh]
-        return remote(place, place, x_ssem.at[d - 1], x_rsem.at[j, d - 1], x_peer(d))
-
-    def x_recv(j, d):
-        place = states.at[j, lax.rem(sh - d + Y, Y)]
-        return remote(place, place, x_ssem.at[d - 1], x_rsem.at[j, d - 1], x_peer(d))
+        return remote(place, place, x_ssem.at[d - 1], x_rsem, x_peer(d))
 
     def x_forward(j):
         @pl.when(jnp.logical_not(from_self(j)))
@@ -151,9 +143,8 @@
     for side in (zh, 1 - zh):
         for i in range(Y):
             x_forward(side * Y + i)
-    for j in range(2 * Y):
-        for d in range(1, Y):
-            x_recv(j, d).wait_recv()
+    others = states.at[:, pl.ds(0, Y - 1)]
+    remote(others, others, x_ssem.at[0], x_rsem, x_peer(1)).wait_recv()
 
     half = tokens // 2
 
@@ -166,21 +157,21 @@
     def half_send(c, i):
         return remote(
             part.at[c, :, lax.rem(y + 2, Y), pl.ds(i * half, half)], half_in.at[c, i],
-            half_ssem, half_rsem.at[c, i], y_to(i),
+            half_ssem, half_rsem.at[c], y_to(i),
         )
 
     def soon_send(c, i):
         rows = pl.ds((1 - i) * half, half)
         return remote(
             part.at[c, :, y_next(i), rows], part_in.at[c, i, :, rows],
-            soon_ssem, soon_rsem.at[c, i], y_to(i),
+            part_ssem, part_rsem.at[c], y_to(i),
         )
 
     def late_send(c, i):
         rows = pl.ds(i * half, half)
         return remote(
             part.at[c, :, y_next(i), rows], part_in.at[c, i, :, rows],
-            late_ssem, late_rsem.at[c, i], y_to(i),
+            part_ssem, part_rsem.at[c], y_to(i),
         )
 
     def cross_send(c):
@@ -196,23 +187,14 @@
 
     def gy_send(c, side, i):
         place = grads.at[c, side, y]
-        at = 2 * side + i
-        return remote(place, place, gy_ssem, gy_rsem.at[c, at], y_to(i))
-
-    def gy_recv(c, side, i):
-        place = grads.at[c, side, y_next(1 - i)]
-        at = 2 * side + i
-        return remote(place, place, gy_ssem, gy_rsem.at[c, at], y_to(i))
+        return remote(place, place, gy_ssem, gy_rsem.at[c, side], y_to(i))
+
+    def arrived(ref, rsem):
+        remote(ref, ref, cross_ssem, rsem, z_peer).wait_recv()
 
     def relay_send(c, side, i):
         place = grads.at[c, side, y_next(1 - i), pl.ds(i * half, half)]
-        at = 2 * side + i
-        return remote(place, place, relay_ssem, relay_rsem.at[c, at], y_to(i))
-
-    def relay_recv(c, side, i):
-        place = grads.at[c, side, lax.rem(y + 2, Y), pl.ds(i * half, half)]
-        at = 2 * side + i
-        return remote(place, place, relay_ssem, relay_rsem.at[c, at], y_to(i))
+        return remote(place, place, relay_ssem, relay_rsem.at[c], y_to(i))
 
     def core_send(c):
         return remote(
@@ -231,7 +213,7 @@
 
     def store(c):
         cols = pl.ds(pl.multiple_of(c * cw, cw), cw)
-        return pltpu.make_async_copy(result.at[c], out.at[:, cols], out_sem.at[c])
+        return pltpu.make_async_copy(result.at[c], out.at[:, cols], out_sem)
 
     def product(c):
         load_w(c).wait()
@@ -250,8 +232,8 @@
             soon_send(c, i).start()
 
     def add_half(c):
-        for i in range(2):
-            half_send(c, i).wait_recv()
+        arrived(half_in.at[c], half_rsem.at[c])
+        for i in range(2):
             rows = pl.ds(i * half, half)
             part[c, :, y_next(i), rows] = (
                 part[c, :, y_next(i), rows].astype(jnp.float32)
@@ -271,9 +253,7 @@
         lax.fori_loop(first, last, some, 0)
 
     def add_up(c):
-        for i in range(2):
-            soon_send(c, i).wait_recv()
-            late_send(c, i).wait_recv()
+        arrived(part_in.at[c], part_rsem.at[c])
 
         def total(side):
             acc = part[c, side, y].astype(jnp.float32)
@@ -286,20 +266,19 @@
         own[c] = total(zh)
 
     def gradient(c):
-        load_cot(c).wait()
         cross_send(c).wait_recv()
         pre = (own[c] + cross_in[c].astype(jnp.float32)) * scale
         sig = jax.nn.sigmoid(pre)
         grads[c, zh, y] = (
-            cot[c].astype(jnp.float32) * sig * (1.0 + pre * (1.0 - sig))
+            cot[:, pl.ds(pl.multiple_of(c * cw, cw), cw)].astype(jnp.float32) * sig * (1.0 + pre * (1.0 - sig))
         ).astype(jnp.bfloat16)
         gz_send(c).start()
         for i in range(2):
             gy_send(c, zh, i).start()
 
     def relay(c, side):
-        for i in range(2):
-            gy_recv(c, side, i).wait_recv()
+        arrived(grads.at[c, side, pl.ds(0, 2)], gy_rsem.at[c, side])
+        for i in range(2):
             relay_send(c, side, i).start()
 
     def pass_on(c):
@@ -312,9 +291,7 @@
         relay(c, 1 - zh)
 
     def fishers(c):
-        for side in range(2):
-            for i in range(2):
-                relay_recv(c, side, i).wait_recv()
+        arrived(grads.at[c, 0, pl.ds(0, 2)], relay_rsem.at[c])
 
         def some(r, carry):
             rows = pl.ds(pl.multiple_of(r * ROWS_AT_ONCE, ROWS_AT_ONCE), ROWS_AT_ONCE)
@@ -385,6 +362,7 @@
 
         return carry
 
+    load_cot.wait()
     lax.fori_loop(0, chunks + LAG_FAR, step, 0)
 
     for b in range(2):
@@ -400,8 +378,7 @@
     for i in range(1, Y):
         sent(states.at[:, 0], x_ssem.at[i - 1])
     sent(half_in, half_ssem)
-    sent(half_in, soon_ssem)
-    sent(half_in, late_ssem)
+    sent(part_in, part_ssem)
     sent(cross, cross_ssem)
     sent(cross, gz_ssem)
     sent(part_in, gy_ssem)
@@ -410,11 +387,7 @@
     sent(near_in, near_ssem)
     sent(far_in, far_ssem)
 
-    def finish(c, carry):
-        store(c).wait()
-        return carry
-
-    lax.fori_loop(0, chunks, finish, 0)
+    pltpu.make_async_copy(out, out, out_sem).wait()
 
 
 def shards(hidden, cotangent, weights, segments):
@@ -426,7 +399,7 @@
     dma = pltpu.SemaphoreType.DMA
     buffers = [
         pltpu.VMEM((n, block_rows, cw), bf),
-        pltpu.VMEM((n, tokens, cw), bf),
+        pltpu.VMEM((tokens, columns), bf),
         pltpu.VMEM((2 * Y, Y, tokens // Y, block_rows), bf),
         pltpu.VMEM((2 * Y * EX, block_rows, tokens), bf),
         pltpu.VMEM((n, 2, Y, tokens, cw), bf),
@@ -443,10 +416,10 @@
         pltpu.VMEM((n, per, cw), bf),
         pltpu.VMEM((block_rows, cw), f32),
     ]
-    one, two, four = ([dma, dma((n,) + more)] for more in ((), (2,), (4,)))
-    crossing = [dma((2 * Y,))] * 2 + [dma((Y - 1,)), dma((2 * Y, Y - 1))]
-    sems = [dma((2 * n,))] + crossing + [dma((n,))]
-    sems += two + two + two + one + one + four + four + one + one + one
+    one, two = [dma, dma((n,))], [dma, dma((n, 2))]
+    crossing = [dma((2 * Y,))] * 2 + [dma((Y - 1,)), dma]
+    sems = [dma((n,)), dma] + crossing + [dma]
+    sems += one + one + one + one + two + one + one + one + one
     return pl.pallas_call(
         kernel,
         out_shape=jax.ShapeDtypeStruct((per, columns), bf),

time: 200 us -> 199 us (level)
  no operation moved by 1% of the time
where the time goes in v4:
time: 199 us; the launch traced here: 198 us
  Pallas kernels  196 us (98%)
    pallas_call x1, Pallas kernels, shards(): pl.pallas_call(kernel, out_shape=jax.ShapeDtypeStruct((per, columns), bf)...  196 us

profile of v4, /device:TPU:2, one launch (start us, length us, event | category | flops | bytes accessed | tf_op | source)
XLA Modules:
  0.0 197.7 jit_solution(3670740018091335946)
XLA Ops:
  0.0 195.9 %shard_map.46 = bf16[64,3584]{1,0:T(8,128)(2,1)} custom-call(bf16[1,128,1024]{2,1,0:T(8,128)(2,1)} %hidden.1, bf16[1,128,3584]{2,1,0:T(8,128)(2,1)} %cotangent.1, bf16[1,512,3584]{2,1,0:T(8,128)(2,1)} %weights.1, s32[8,128]{1,0:T(8,128)} %segments.1), custom_call_target="tpu_custom_call" | custom-call | tf_op jit(solution)/shard_map/pallas_call | solution.py:423
  195.9 1.8 copy.6

commit v5 on v4

--- a/solution.py
+++ b/solution.py
@@ -10,9 +10,10 @@
 EX = 3
 Y = 4
 CHUNK = 256
+DIRECT = 4
 ROWS_AT_ONCE = 64
 LAG_HALF, LAG_SUM, LAG_GRAD, LAG_PASS, LAG_RELAY = 1, 2, 4, 6, 7
-LAG_FISHER, LAG_CORE, LAG_NEAR, LAG_FAR = 8, 9, 10, 11
+LAG_FISHER, LAG_CORE, LAG_NEAR, LAG_FAR = 8, 9, 11, 12
 
 
 def kernel(
@@ -27,6 +28,7 @@
     chunks, block_rows, cw = w.shape
     tokens = cot.shape[0]
     quarter = tokens // Y
+    relayed = chunks - DIRECT
     scale = 1.0 / math.sqrt(block_rows * 2 * Y)
     mp, dp, sh = lax.axis_index("mp"), lax.axis_index("dp"), lax.axis_index("shard")
     core, b0, b1 = lax.rem(mp, 2), lax.rem(mp // 2, 2), mp // 4
@@ -79,7 +81,7 @@
     def to_self(b, q):
         return jnp.logical_and(dp == 2 * sh + b, sh == q)
 
-    peers = [y_peer(1), y_peer(3), x_peer(1), x_peer(2), x_peer(3)]
+    peers = [y_peer(1), y_peer(2), y_peer(3), x_peer(1), x_peer(2), x_peer(3)]
     peers += [z_peer, core_peer, near_peer, far_peer]
     for device in peers:
         greet(device)
@@ -195,6 +197,19 @@
     def relay_send(c, side, i):
         place = grads.at[c, side, y_next(1 - i), pl.ds(i * half, half)]
         return remote(place, place, relay_ssem, relay_rsem.at[c], y_to(i))
+
+    def direct_send(c, side, i):
+        place = grads.at[c, side, y, pl.ds(i * half, half)]
+        return remote(place, place, relay_ssem, relay_rsem.at[c], y_peer(2))
+
+    def spread(c, side):
+        for i in range(2):
+            gy_send(c, side, i).start()
+
+        @pl.when(c >= relayed)
+        def _():
+            for i in range(2):
+                direct_send(c, side, i).start()
 
     def core_send(c):
         return remote(
@@ -273,18 +288,19 @@
             cot[:, pl.ds(pl.multiple_of(c * cw, cw), cw)].astype(jnp.float32) * sig * (1.0 + pre * (1.0 - sig))
         ).astype(jnp.bfloat16)
         gz_send(c).start()
-        for i in range(2):
-            gy_send(c, zh, i).start()
+        spread(c, zh)
 
     def relay(c, side):
         arrived(grads.at[c, side, pl.ds(0, 2)], gy_rsem.at[c, side])
-        for i in range(2):
-            relay_send(c, side, i).start()
+
+        @pl.when(c < relayed)
+        def _():
+            for i in range(2):
+                relay_send(c, side, i).start()
 
     def pass_on(c):
         gz_recv(c).wait_recv()
-        for i in range(2):
-            gy_send(c, 1 - zh, i).start()
+        spread(c, 1 - zh)
         relay(c, zh)
 
     def relay_far(c):
@@ -350,11 +366,27 @@
 
     def step(t, carry):
         for stage, lag in stages:
-            c = t - lag
-
-            @pl.when(jnp.logical_and(c >= 0, c < chunks))
-            def _():
-                stage(c)
+            if lag < LAG_FISHER:
+                c = t - lag
+
+                @pl.when(jnp.logical_and(c >= 0, c < chunks))
+                def _():
+                    stage(c)
+
+            else:
+
+                def run(u, carry):
+                    c = t - lag + u
+                    runs = jnp.logical_and(u == 0, jnp.logical_and(c >= 0, c < relayed))
+                    direct = jnp.logical_and(u == 1, jnp.logical_and(c >= relayed, c < chunks))
+
+                    @pl.when(jnp.logical_or(runs, direct))
+                    def _():
+                        stage(c)
+
+                    return carry
+
+                lax.fori_loop(0, 2, run, 0)
 
         @pl.when(jnp.logical_and(t >= 1, t <= Y))
         def _():
@@ -363,7 +395,7 @@
         return carry
 
     load_cot.wait()
-    lax.fori_loop(0, chunks + LAG_FAR, step, 0)
+    lax.fori_loop(0, chunks + LAG_FAR - 1, step, 0)
 
     for b in range(2):
         for q in range(Y):

time: 199 us -> 197 us (0.990)
  Pallas kernels: 196 us -> 194 us
    pallas_call x1, Pallas kernels: 196 us -> 194 us  [shards(): pl.pallas_call(kernel, out_shape=jax.ShapeDtypeStruct((per, columns), bf)...]
where the time goes in v5:
time: 197 us; the launch traced here: 196 us
  Pallas kernels  194 us (98%)
    pallas_call x1, Pallas kernels, shards(): pl.pallas_call(kernel, out_shape=jax.ShapeDtypeStruct((per, columns), bf)...  194 us

profile of v5, /device:TPU:2, one launch (start us, length us, event | category | flops | bytes accessed | tf_op | source)
XLA Modules:
  0.0 195.7 jit_solution(12826637464516399704)
XLA Ops:
  0.0 193.9 %shard_map.46 = bf16[64,3584]{1,0:T(8,128)(2,1)} custom-call(bf16[1,128,1024]{2,1,0:T(8,128)(2,1)} %hidden.1, bf16[1,128,3584]{2,1,0:T(8,128)(2,1)} %cotangent.1, bf16[1,512,3584]{2,1,0:T(8,128)(2,1)} %weights.1, s32[8,128]{1,0:T(8,128)} %segments.1), custom_call_target="tpu_custom_call" | custom-call | tf_op jit(solution)/shard_map/pallas_call | solution.py:455
  193.9 1.8 copy.6

commit v6 on v5

--- a/solution.py
+++ b/solution.py
@@ -11,6 +11,7 @@
 Y = 4
 CHUNK = 256
 DIRECT = 4
+EARLY = 4
 ROWS_AT_ONCE = 64
 LAG_HALF, LAG_SUM, LAG_GRAD, LAG_PASS, LAG_RELAY = 1, 2, 4, 6, 7
 LAG_FISHER, LAG_CORE, LAG_NEAR, LAG_FAR = 8, 9, 11, 12
@@ -128,7 +129,7 @@
 
     def x_send(j, d):
         place = states.at[j, sh]
-        return remote(place, place, x_ssem.at[d - 1], x_rsem, x_peer(d))
+        return remote(place, place, x_ssem.at[d - 1], x_rsem.at[j // Y], x_peer(d))
 
     def x_forward(j):
         @pl.when(jnp.logical_not(from_self(j)))
@@ -145,8 +146,28 @@
     for side in (zh, 1 - zh):
         for i in range(Y):
             x_forward(side * Y + i)
-    others = states.at[:, pl.ds(0, Y - 1)]
-    remote(others, others, x_ssem.at[0], x_rsem, x_peer(1)).wait_recv()
+    def x_arrived(side):
+        others = states.at[pl.ds(side * Y, Y), pl.ds(0, Y - 1)]
+        remote(others, others, x_ssem.at[0], x_rsem.at[side], x_peer(1)).wait_recv()
+
+    def products(c, side):
+        def some(j, carry):
+            rows = states[side * Y + j].reshape(tokens, block_rows)
+            part[c, side, j] = jnp.dot(
+                rows, w[c], preferred_element_type=jnp.float32
+            ).astype(jnp.bfloat16)
+            return carry
+
+        lax.fori_loop(0, Y, some, 0)
+
+    def early(c, carry):
+        load_w(c).wait()
+        products(c, zh)
+        return carry
+
+    x_arrived(zh)
+    lax.fori_loop(0, EARLY, early, 0)
+    x_arrived(1 - zh)
 
     half = tokens // 2
 
@@ -231,16 +252,11 @@
         return pltpu.make_async_copy(result.at[c], out.at[:, cols], out_sem)
 
     def product(c):
-        load_w(c).wait()
-
-        def some(j, carry):
-            rows = states[j].reshape(tokens, block_rows)
-            part[c, j // Y, lax.rem(j, Y)] = jnp.dot(
-                rows, w[c], preferred_element_type=jnp.float32
-            ).astype(jnp.bfloat16)
-            return carry
-
-        lax.fori_loop(0, 2 * Y, some, 0)
+        @pl.when(c >= EARLY)
+        def _():
+            early(c, 0)
+
+        products(c, 1 - zh)
         for i in range(2):
             half_send(c, i).start()
         for i in range(2):
@@ -449,7 +465,7 @@
         pltpu.VMEM((block_rows, cw), f32),
     ]
     one, two = [dma, dma((n,))], [dma, dma((n, 2))]
-    crossing = [dma((2 * Y,))] * 2 + [dma((Y - 1,)), dma]
+    crossing = [dma((2 * Y,))] * 2 + [dma((Y - 1,)), dma((2,))]
     sems = [dma((n,)), dma] + crossing + [dma]
     sems += one + one + one + one + two + one + one + one + one
     return pl.pallas_call(

time: 197 us -> 196 us (level)
  no operation moved by 1% of the time
where the time goes in v6:
time: 196 us; the launch traced here: 195 us
  Pallas kernels  193 us (98%)
    pallas_call x1, Pallas kernels, shards(): pl.pallas_call(kernel, out_shape=jax.ShapeDtypeStruct((per, columns), bf)...  193 us

profile of v6, /device:TPU:2, one launch (start us, length us, event | category | flops | bytes accessed | tf_op | source)
XLA Modules:
  0.0 195.1 jit_solution(9625648439362104618)
XLA Ops:
  0.0 193.3 %shard_map.46 = bf16[64,3584]{1,0:T(8,128)(2,1)} custom-call(bf16[1,128,1024]{2,1,0:T(8,128)(2,1)} %hidden.1, bf16[1,128,3584]{2,1,0:T(8,128)(2,1)} %cotangent.1, bf16[1,512,3584]{2,1,0:T(8,128)(2,1)} %weights.1, s32[8,128]{1,0:T(8,128)} %segments.1), custom_call_target="tpu_custom_call" | custom-call | tf_op jit(solution)/shard_map/pallas_call | solution.py:471
  193.3 1.8 copy.6
